TPU v7x, 32 devices: a whole 2x2x4 slice. The times are simulated.
32 devices in a mesh: ma: 4 (over y, x), af: 8 (over z, core).
Axes of the slice: x: 2, y: 2, z: 4, core: 2. Of those that a mesh axis runs over, the one named last changes fastest.
Arguments:
- beams: bfloat16 [4, 8, 4, 512, 2048], P(None, 'af', 'ma'), may hold values from -2 to 2
- spectrum: float32 [32, 3, 1024], P('af'), may hold values from 0.3 to 3
- partners: int32 [32, 3], P('af'), may hold values from 0 to 31, as said below
Outputs:
- covariance: bfloat16 [4, 32, 3, 2, 512, 512], P('ma', 'af')
Inputs may be any that keep to these rules, and one draw needn't show every extreme that they name: partners[c, k] lies in the band of c (channels 64 * (c // 64) up to the band's end or the last channel) and at most 2 channels from c; the distance 2 occurs.
All inputs are finite; a program needn't handle non-finite values.
Results may differ from a plain program's by a relative error of at most 0.0044.
Values may be sent and summed in bfloat16 or wider, within the bound.
A program may use at most 192 MiB of HBM per device.

v0:
```python
import jax
import jax.numpy as jnp
from jax import lax
from jax.sharding import PartitionSpec as P


def from_behind(array, axis, by):
    count = lax.axis_size(axis)
    pairs = [(i, i + by) for i in range(count) if 0 <= i + by < count]
    return lax.ppermute(array, axis, pairs)


def sandwich(own, right, weights):
    half = own.shape[-1] // 2
    real_part = own[:, :half].astype(jnp.float32) * weights
    imag_part = own[:, half:].astype(jnp.float32) * weights
    upper = jnp.concatenate([real_part, imag_part], axis=1)
    lower = jnp.concatenate([imag_part, -real_part], axis=1)
    left = jnp.concatenate([upper, lower], axis=0).astype(jnp.bfloat16)
    product = lax.dot_general(
        left, right, (((1,), (1,)), ((), ())), preferred_element_type=jnp.float32
    )
    return product.astype(jnp.bfloat16).reshape(2, own.shape[0], own.shape[0])


def body(beams, spectrum, partners):
    moved = lax.all_to_all(beams, "ma", split_axis=0, concat_axis=2, tiled=True)
    m_dev, groups, per_group, rows, width = moved.shape
    chans = groups * per_group
    local = moved.reshape(m_dev, chans, rows, width)
    base = lax.axis_index("af") * chans
    below = from_behind(local, "af", 1)
    above = from_behind(local, "af", -1)
    extended = jnp.concatenate([below, local, above], axis=1)
    slots = partners.shape[1]
    blocks = local[0]
    beside_all = extended[0]

    def one_channel(channel):
        own = lax.dynamic_index_in_dim(blocks, channel, 0, keepdims=False)
        weights = lax.dynamic_index_in_dim(spectrum, channel, 0, keepdims=False)
        targets = lax.dynamic_index_in_dim(partners, channel, 0, keepdims=False)
        outs = []
        for slot in range(slots):
            where = targets[slot] - base + chans
            right = lax.dynamic_index_in_dim(beside_all, where, 0, keepdims=False)
            outs.append(sandwich(own, right, weights[slot]))
        return jnp.stack(outs, axis=0)

    results = [lax.map(one_channel, jnp.arange(chans, dtype=jnp.int32))]
    return jnp.stack(results, axis=0)


def solution(mesh):
    in_specs = (P(None, "af", "ma", None, None), P("af", None, None), P("af", None))
    out_specs = P("ma", "af", None, None, None, None)
    return jax.shard_map(body, mesh=mesh, in_specs=in_specs, out_specs=out_specs, check_vma=False)
```

profile of v0, /device:TPU:1, one launch (start us, length us, event | category | flops | bytes accessed | tf_op | source)
XLA Modules:
  0.0 341.0 jit_solution(14998978462991245753)
XLA Ops:
  0.0 100.3 %all_to_all.4 = bf16[4,1,1,512,2048]{4,3,2,1,0:T(8,128)(2,1)} all-to-all(bf16[4,1,1,512,2048]{4,3,2,1,0:T(8,128)(2,1)} %param.5), channel_id=1, replica_groups=mesh['ma'=4,'af'=8] {'ma'}, dimensions={0} | all-to-all | bytes 16777216 | tf_op jit(solution)/shard_map/all_to_all | solution.py:27
  100.3 4.9 %collective-permute-start = (bf16[1,4,512,2048]{3,2,1,0:T(8,128)(2,1)}, bf16[1,4,512,2048]{3,2,1,0:T(8,128)(2,1)}, u32[]{:S(2)}, u32[]{:S(2)}) collective-permute-start(bf16[1,4,512,2048]{3,2,1,0:T(8,128)(2,1)} %bitcast.16), channel_id=1, source_target_pairs={{0,1},{1,2},{2,3},{3,4},{4,5},{5,6},{6,7},{8,9},{9,10},{10,11},{11... | collective-permute-start | bytes 25165832 | tf_op jit(solution)/shard_map/ppermute | solution.py:10
  105.1 3.1 collective-permute-start.1
  108.3 87.6 %collective-permute-done = bf16[1,4,512,2048]{3,2,1,0:T(8,128)(2,1)} collective-permute-done((bf16[1,4,512,2048]{3,2,1,0:T(8,128)(2,1)}, bf16[1,4,512,2048]{3,2,1,0:T(8,128)(2,1)}, u32[]{:S(2)}, u32[]{:S(2)}) %collective-permute-start) | collective-permute-done | bytes 8388640 | tf_op jit(solution)/shard_map/ppermute | solution.py:10
  195.8 4.4 %collective-permute-done.1 = bf16[1,4,512,2048]{3,2,1,0:T(8,128)(2,1)} collective-permute-done((bf16[1,4,512,2048]{3,2,1,0:T(8,128)(2,1)}, bf16[1,4,512,2048]{3,2,1,0:T(8,128)(2,1)}, u32[]{:S(2)}, u32[]{:S(2)}) %collective-permute-start.1) | collective-permute-done | bytes 8388640 | tf_op jit(solution)/shard_map/ppermute | solution.py:10
  200.2 17.5 %maximum_bitcast_fusion.1 = bf16[12,512,2048]{2,1,0:T(8,128)(2,1)} fusion(bf16[1,4,512,2048]{3,2,1,0:T(8,128)(2,1)} %collective-permute-done.1, bf16[1,4,512,2048]{3,2,1,0:T(8,128)(2,1)} %bitcast.16, bf16[1,4,512,2048]{3,2,1,0:T(8,128)(2,1)} %collective-permute-done), kind=kLoop, calls=%fused_computation.64 | loop fusion | flops 25165824 | bytes 50331648 | tf_op jit(solution)/shard_map/squeeze | solution.py:37
  217.8 123.2 %while.13 = (s32[]{:T(128)}, bf16[4,3,2,512,512]{4,3,2,1,0:T(8,128)(2,1)}, s32[4]{0:T(128)S(1)}, bf16[4,512,2048]{2,1,0:T(8,128)(2,1)}, f32[4,3,1024]{2,0,1:T(4,...) while((s32[]{:T(128)}, ...), condition=%wide.region_1.2_spmd, body=%wide.region_0.1_spmd.sunk | while | flops 6514278400 | bytes 49320956 | solution.py:50
  217.8 0.6 dynamic_slice.85
  220.0 0.8 constant_dynamic-slice_fusion.7
  220.8 1.7 dynamic-slice_bitcast_fusion.2
  222.5 4.1 %fusion.84 = (bf16[512,1024]{1,0:T(8,128)(2,1)}, bf16[512,1024]{1,0:T(8,128)(2,1)}, bf16[512,1024]{1,0:T(8,128)(2,1)}, bf16[512,1024]{1,0:T(8,128)(2,1)S(1)}, bf...) fusion(f32[1024]{0:T(1024)S(1)} %bitcast.69, ...), kind=kLoop, calls=%fused_computation.33.clone.1 | loop fusion | flops 10485760 | bytes 11546624 | tf_op jit(solution)/shard_map/convert.16
  226.6 0.7 constant_dynamic-slice_fusion.6
  227.3 0.6 fusion.83
  228.6 6.2 %fusion.87 = bf16[1024,512]{1,0:T(8,128)(2,1)} fusion(bf16[12,512,2048]{2,1,0:T(8,128)(2,1)} %get-tuple-element.281, s32[]{:T(128)S(6)} %select_n.41, bf16[512,1024]{1,0:T(8,128)(2,1)} %get-tuple-element.243, bf16[512,1024]{1,0:T(8,128)(2,1)} %get-tuple-element.244, bf16[512,1024]{1,0:T(8,128)(2,1)} %get-tuple-element.245), kind=kOutput, calls=%fused_computation.53.clone.1 | convolution fusion | flops 2164785152 | bytes 6291460 | tf_op jit(solution)/shard_map/while/body/eval_jaxpr/dot_general | solution.py:20
  235.5 6.3 %fusion.86 = bf16[1024,512]{1,0:T(8,128)(2,1)} fusion(bf16[12,512,2048]{2,1,0:T(8,128)(2,1)} %get-tuple-element.281, s32[]{:T(128)S(6)} %select_n.40, bf16[512,1024]{1,0:T(8,128)(2,1)} %get-tuple-element.239, bf16[512,1024]{1,0:T(8,128)(2,1)} %get-tuple-element.240, bf16[512,1024]{1,0:T(8,128)(2,1)} %get-tuple-element.241), kind=kOutput, calls=%fused_computation.52.clone.1 | convolution fusion | flops 2164785152 | bytes 6291460 | tf_op jit(solution)/shard_map/while/body/eval_jaxpr/dot_general | solution.py:20
  242.4 4.1 %fusion.85 = bf16[1024,512]{1,0:T(8,128)(2,1)S(1)} fusion(bf16[12,512,2048]{2,1,0:T(8,128)(2,1)} %get-tuple-element.281, s32[]{:T(128)S(6)} %select_n.39, bf16[512,1024]{1,0:T(8,128)(2,1)S(1)} %get-tuple-element.235, bf16[512,1024]{1,0:T(8,128)(2,1)S(1)} %get-tuple-element.236, bf16[512,1024]{1,0:T(8,128)(2,1)S(1)} %get-tuple-element.237), kind=kOutput, calls=%fused_computation.51.clone.1 | convolution fusion | flops 2164785152 | bytes 6291460 | tf_op jit(solution)/shard_map/while/body/eval_jaxpr/dot_general | solution.py:20
  246.5 2.1 fusion.88
  248.6 0.6 dynamic_slice.85
  250.8 0.8 constant_dynamic-slice_fusion.7
  251.6 1.7 dynamic-slice_bitcast_fusion.2
  253.3 4.1 %fusion.84 = (bf16[512,1024]{1,0:T(8,128)(2,1)}, bf16[512,1024]{1,0:T(8,128)(2,1)}, bf16[512,1024]{1,0:T(8,128)(2,1)}, bf16[512,1024]{1,0:T(8,128)(2,1)S(1)}, bf...) fusion(f32[1024]{0:T(1024)S(1)} %bitcast.69, ...), kind=kLoop, calls=%fused_computation.33.clone.1 | loop fusion | flops 10485760 | bytes 11546624 | tf_op jit(solution)/shard_map/convert.16
  257.4 0.7 constant_dynamic-slice_fusion.6
  258.1 0.6 fusion.83
  259.4 6.2 %fusion.87 = bf16[1024,512]{1,0:T(8,128)(2,1)} fusion(bf16[12,512,2048]{2,1,0:T(8,128)(2,1)} %get-tuple-element.281, s32[]{:T(128)S(6)} %select_n.41, bf16[512,1024]{1,0:T(8,128)(2,1)} %get-tuple-element.243, bf16[512,1024]{1,0:T(8,128)(2,1)} %get-tuple-element.244, bf16[512,1024]{1,0:T(8,128)(2,1)} %get-tuple-element.245), kind=kOutput, calls=%fused_computation.53.clone.1 | convolution fusion | flops 2164785152 | bytes 6291460 | tf_op jit(solution)/shard_map/while/body/eval_jaxpr/dot_general | solution.py:20
  266.3 6.3 %fusion.86 = bf16[1024,512]{1,0:T(8,128)(2,1)} fusion(bf16[12,512,2048]{2,1,0:T(8,128)(2,1)} %get-tuple-element.281, s32[]{:T(128)S(6)} %select_n.40, bf16[512,1024]{1,0:T(8,128)(2,1)} %get-tuple-element.239, bf16[512,1024]{1,0:T(8,128)(2,1)} %get-tuple-element.240, bf16[512,1024]{1,0:T(8,128)(2,1)} %get-tuple-element.241), kind=kOutput, calls=%fused_computation.52.clone.1 | convolution fusion | flops 2164785152 | bytes 6291460 | tf_op jit(solution)/shard_map/while/body/eval_jaxpr/dot_general | solution.py:20
  273.2 4.1 %fusion.85 = bf16[1024,512]{1,0:T(8,128)(2,1)S(1)} fusion(bf16[12,512,2048]{2,1,0:T(8,128)(2,1)} %get-tuple-element.281, s32[]{:T(128)S(6)} %select_n.39, bf16[512,1024]{1,0:T(8,128)(2,1)S(1)} %get-tuple-element.235, bf16[512,1024]{1,0:T(8,128)(2,1)S(1)} %get-tuple-element.236, bf16[512,1024]{1,0:T(8,128)(2,1)S(1)} %get-tuple-element.237), kind=kOutput, calls=%fused_computation.51.clone.1 | convolution fusion | flops 2164785152 | bytes 6291460 | tf_op jit(solution)/shard_map/while/body/eval_jaxpr/dot_general | solution.py:20
  277.3 2.1 fusion.88
  279.4 0.6 dynamic_slice.85
  281.6 0.8 constant_dynamic-slice_fusion.7
  282.4 1.7 dynamic-slice_bitcast_fusion.2
  284.1 4.1 %fusion.84 = (bf16[512,1024]{1,0:T(8,128)(2,1)}, bf16[512,1024]{1,0:T(8,128)(2,1)}, bf16[512,1024]{1,0:T(8,128)(2,1)}, bf16[512,1024]{1,0:T(8,128)(2,1)S(1)}, bf...) fusion(f32[1024]{0:T(1024)S(1)} %bitcast.69, ...), kind=kLoop, calls=%fused_computation.33.clone.1 | loop fusion | flops 10485760 | bytes 11546624 | tf_op jit(solution)/shard_map/convert.16
  288.2 0.7 constant_dynamic-slice_fusion.6
  288.9 0.6 fusion.83
  290.2 6.2 %fusion.87 = bf16[1024,512]{1,0:T(8,128)(2,1)} fusion(bf16[12,512,2048]{2,1,0:T(8,128)(2,1)} %get-tuple-element.281, s32[]{:T(128)S(6)} %select_n.41, bf16[512,1024]{1,0:T(8,128)(2,1)} %get-tuple-element.243, bf16[512,1024]{1,0:T(8,128)(2,1)} %get-tuple-element.244, bf16[512,1024]{1,0:T(8,128)(2,1)} %get-tuple-element.245), kind=kOutput, calls=%fused_computation.53.clone.1 | convolution fusion | flops 2164785152 | bytes 6291460 | tf_op jit(solution)/shard_map/while/body/eval_jaxpr/dot_general | solution.py:20
  297.1 6.3 %fusion.86 = bf16[1024,512]{1,0:T(8,128)(2,1)} fusion(bf16[12,512,2048]{2,1,0:T(8,128)(2,1)} %get-tuple-element.281, s32[]{:T(128)S(6)} %select_n.40, bf16[512,1024]{1,0:T(8,128)(2,1)} %get-tuple-element.239, bf16[512,1024]{1,0:T(8,128)(2,1)} %get-tuple-element.240, bf16[512,1024]{1,0:T(8,128)(2,1)} %get-tuple-element.241), kind=kOutput, calls=%fused_computation.52.clone.1 | convolution fusion | flops 2164785152 | bytes 6291460 | tf_op jit(solution)/shard_map/while/body/eval_jaxpr/dot_general | solution.py:20
  304.0 4.1 %fusion.85 = bf16[1024,512]{1,0:T(8,128)(2,1)S(1)} fusion(bf16[12,512,2048]{2,1,0:T(8,128)(2,1)} %get-tuple-element.281, s32[]{:T(128)S(6)} %select_n.39, bf16[512,1024]{1,0:T(8,128)(2,1)S(1)} %get-tuple-element.235, bf16[512,1024]{1,0:T(8,128)(2,1)S(1)} %get-tuple-element.236, bf16[512,1024]{1,0:T(8,128)(2,1)S(1)} %get-tuple-element.237), kind=kOutput, calls=%fused_computation.51.clone.1 | convolution fusion | flops 2164785152 | bytes 6291460 | tf_op jit(solution)/shard_map/while/body/eval_jaxpr/dot_general | solution.py:20
  308.1 0.0 copy-done
  308.1 2.1 fusion.88
  310.2 0.6 dynamic_slice.85
  312.4 0.8 constant_dynamic-slice_fusion.7
  313.1 1.7 dynamic-slice_bitcast_fusion.2
  314.9 4.1 %fusion.84 = (bf16[512,1024]{1,0:T(8,128)(2,1)}, bf16[512,1024]{1,0:T(8,128)(2,1)}, bf16[512,1024]{1,0:T(8,128)(2,1)}, bf16[512,1024]{1,0:T(8,128)(2,1)S(1)}, bf...) fusion(f32[1024]{0:T(1024)S(1)} %bitcast.69, ...), kind=kLoop, calls=%fused_computation.33.clone.1 | loop fusion | flops 10485760 | bytes 11546624 | tf_op jit(solution)/shard_map/convert.16
  319.0 0.7 constant_dynamic-slice_fusion.6
  319.7 0.6 fusion.83
  321.0 6.2 %fusion.87 = bf16[1024,512]{1,0:T(8,128)(2,1)} fusion(bf16[12,512,2048]{2,1,0:T(8,128)(2,1)} %get-tuple-element.281, s32[]{:T(128)S(6)} %select_n.41, bf16[512,1024]{1,0:T(8,128)(2,1)} %get-tuple-element.243, bf16[512,1024]{1,0:T(8,128)(2,1)} %get-tuple-element.244, bf16[512,1024]{1,0:T(8,128)(2,1)} %get-tuple-element.245), kind=kOutput, calls=%fused_computation.53.clone.1 | convolution fusion | flops 2164785152 | bytes 6291460 | tf_op jit(solution)/shard_map/while/body/eval_jaxpr/dot_general | solution.py:20
  327.8 6.3 %fusion.86 = bf16[1024,512]{1,0:T(8,128)(2,1)} fusion(bf16[12,512,2048]{2,1,0:T(8,128)(2,1)} %get-tuple-element.281, s32[]{:T(128)S(6)} %select_n.40, bf16[512,1024]{1,0:T(8,128)(2,1)} %get-tuple-element.239, bf16[512,1024]{1,0:T(8,128)(2,1)} %get-tuple-element.240, bf16[512,1024]{1,0:T(8,128)(2,1)} %get-tuple-element.241), kind=kOutput, calls=%fused_computation.52.clone.1 | convolution fusion | flops 2164785152 | bytes 6291460 | tf_op jit(solution)/shard_map/while/body/eval_jaxpr/dot_general | solution.py:20
  334.8 4.1 %fusion.85 = bf16[1024,512]{1,0:T(8,128)(2,1)S(1)} fusion(bf16[12,512,2048]{2,1,0:T(8,128)(2,1)} %get-tuple-element.281, s32[]{:T(128)S(6)} %select_n.39, bf16[512,1024]{1,0:T(8,128)(2,1)S(1)} %get-tuple-element.235, bf16[512,1024]{1,0:T(8,128)(2,1)S(1)} %get-tuple-element.236, bf16[512,1024]{1,0:T(8,128)(2,1)S(1)} %get-tuple-element.237), kind=kOutput, calls=%fused_computation.51.clone.1 | convolution fusion | flops 2164785152 | bytes 6291460 | tf_op jit(solution)/shard_map/while/body/eval_jaxpr/dot_general | solution.py:20
  338.9 2.1 fusion.88
  (17 shorter events, 0.0 us)
Async XLA Ops:
  100.3 95.6 %collective-permute-start = (bf16[1,4,512,2048]{3,2,1,0:T(8,128)(2,1)}, bf16[1,4,512,2048]{3,2,1,0:T(8,128)(2,1)}, u32[]{:S(2)}, u32[]{:S(2)}) collective-permute-start(bf16[1,4,512,2048]{3,2,1,0:T(8,128)(2,1)} %bitcast.16), channel_id=1, source_target_pairs={{0,1},{1,2},{2,3},{3,4},{4,5},{5,6},{6,7},{8,9},{9,10},{10,11},{11... | collective-permute-start | bytes 25165832 | tf_op jit(solution)/shard_map/ppermute | solution.py:10
  105.1 95.1 %collective-permute-start.1 = (bf16[1,4,512,2048]{3,2,1,0:T(8,128)(2,1)}, bf16[1,4,512,2048]{3,2,1,0:T(8,128)(2,1)}, u32[]{:S(2)}, u32[]{:S(2)}) collective-permute-start(bf16[1,4,512,2048]{3,2,1,0:T(8,128)(2,1)} %bitcast.16), channel_id=1, source_target_pairs={{1,0},{2,1},{3,2},{4,3},{5,4},{6,5},{7,6},{9,8},{10,9},{11,10},{12... | collective-permute-start | bytes 25165832 | tf_op jit(solution)/shard_map/ppermute | solution.py:10
  242.4 4.1 %copy-start = (bf16[1024,512]{1,0:T(8,128)(2,1)S(1)}, bf16[1024,512]{1,0:T(8,128)(2,1)}, u32[]{:S(2)}) copy-start(bf16[1024,512]{1,0:T(8,128)(2,1)} %fusion.87) | copy-start | bytes 3145732 | tf_op jit(solution)/shard_map/while
  242.4 4.1 %copy-start.1 = (bf16[1024,512]{1,0:T(8,128)(2,1)S(1)}, bf16[1024,512]{1,0:T(8,128)(2,1)}, u32[]{:S(2)}) copy-start(bf16[1024,512]{1,0:T(8,128)(2,1)} %fusion.86) | copy-start | bytes 3145732 | tf_op jit(solution)/shard_map/while
  273.2 4.1 %copy-start = (bf16[1024,512]{1,0:T(8,128)(2,1)S(1)}, bf16[1024,512]{1,0:T(8,128)(2,1)}, u32[]{:S(2)}) copy-start(bf16[1024,512]{1,0:T(8,128)(2,1)} %fusion.87) | copy-start | bytes 3145732 | tf_op jit(solution)/shard_map/while
  273.2 4.1 %copy-start.1 = (bf16[1024,512]{1,0:T(8,128)(2,1)S(1)}, bf16[1024,512]{1,0:T(8,128)(2,1)}, u32[]{:S(2)}) copy-start(bf16[1024,512]{1,0:T(8,128)(2,1)} %fusion.86) | copy-start | bytes 3145732 | tf_op jit(solution)/shard_map/while
  304.0 4.1 %copy-start = (bf16[1024,512]{1,0:T(8,128)(2,1)S(1)}, bf16[1024,512]{1,0:T(8,128)(2,1)}, u32[]{:S(2)}) copy-start(bf16[1024,512]{1,0:T(8,128)(2,1)} %fusion.87) | copy-start | bytes 3145732 | tf_op jit(solution)/shard_map/while
  304.0 4.1 %copy-start.1 = (bf16[1024,512]{1,0:T(8,128)(2,1)S(1)}, bf16[1024,512]{1,0:T(8,128)(2,1)}, u32[]{:S(2)}) copy-start(bf16[1024,512]{1,0:T(8,128)(2,1)} %fusion.86) | copy-start | bytes 3145732 | tf_op jit(solution)/shard_map/while
  334.7 4.1 %copy-start = (bf16[1024,512]{1,0:T(8,128)(2,1)S(1)}, bf16[1024,512]{1,0:T(8,128)(2,1)}, u32[]{:S(2)}) copy-start(bf16[1024,512]{1,0:T(8,128)(2,1)} %fusion.87) | copy-start | bytes 3145732 | tf_op jit(solution)/shard_map/while
  334.8 4.1 %copy-start.1 = (bf16[1024,512]{1,0:T(8,128)(2,1)S(1)}, bf16[1024,512]{1,0:T(8,128)(2,1)}, u32[]{:S(2)}) copy-start(bf16[1024,512]{1,0:T(8,128)(2,1)} %fusion.86) | copy-start | bytes 3145732 | tf_op jit(solution)/shard_map/while
where the time goes:
time: 342 us; the launch traced here: 341 us
  blocking collectives  100 us (29%)
  waiting for transfers between devices  92 us (27%)
  matrix products  66.4 us (19%)
  other arithmetic  42.2 us (12%)
  local copies, waits for them, and re-layouts  17.6 us (5%)
  loops' own time  14.4 us (4%)
  starting transfers between devices  7.96 us (2%)
    all_to_all x1, blocking collectives, body(): moved = lax.all_to_all(beams, 'ma', split_axis=0, concat_axis=2, tiled=True)  100 us
    ppermute x2, waiting for transfers between devices, from_behind(): return lax.ppermute(array, axis, pairs)  92 us
    dot_general x12, matrix products, sandwich(): lax.dot_general(left, right, (((1,), (1,)), ((), ())), preferred_element_...  66.4 us
    squeeze x1, other arithmetic, body(): beside_all = extended[0]  17.5 us
    another operation x4, other arithmetic  16.5 us
    another operation x1, loops' own time, body(): results = [lax.map(one_channel, jnp.arange(chans, dtype=jnp.int32))]  14.4 us
    dynamic_update_slice x4, other arithmetic, body(): results = [lax.map(one_channel, jnp.arange(chans, dtype=jnp.int32))]  8.23 us
    ppermute x2, starting transfers between devices, from_behind(): return lax.ppermute(array, axis, pairs)  7.96 us
  transfers between devices with their start and end apart: 2, of which 2 were waited for; matrix products, arithmetic and copies ran while one was open for 0% of the time, Pallas kernels for 0%

commit v1 on v0

v1 whole, which is shorter than its diff:
```python
import functools

import jax
import jax.numpy as jnp
from jax import lax
from jax.experimental import pallas as pl
from jax.experimental.pallas import tpu as pltpu
from jax.sharding import PartitionSpec as P

MESH = pl.DeviceIdType.MESH
REACH = 2
LANES = 128
AHEAD = 3
STAGES = 4


def flip(me, by, count):
    bit = 1
    peer = me
    while bit < count:
        if by & bit:
            peer = peer + bit * (1 - 2 * ((me // bit) % 2))
        bit *= 2
    return peer


def kernel(n_ma, n_af, chunks, partners, beams, spectrum, out, *scratch):
    ext = scratch[:chunks]
    acc, stage, a_send, a_recv, h_send, h_recv, own_sem, out_sem = scratch[chunks:]
    ma = lax.axis_index("ma")
    af = lax.axis_index("af")
    chans = n_ma
    rows = beams.shape[3]
    half = beams.shape[4] // 2
    slots = spectrum.shape[1]
    has_below = af > 0
    has_above = af < n_af - 1

    def remote(chunk, d, part):
        return pltpu.make_async_remote_copy(
            src_ref=beams.at[flip(ma, d, n_ma), 0, 0, :, pl.ds(part * half + chunk * LANES, LANES)],
            dst_ref=ext[chunk].at[REACH + ma, :, pl.ds(part * LANES, LANES)],
            send_sem=a_send.at[chunk, d - 1, part],
            recv_sem=a_recv.at[chunk, d - 1, part],
            device_id=(flip(ma, d, n_ma), af),
            device_id_type=MESH,
        )

    def arriving(chunk, d, part):
        return pltpu.make_async_remote_copy(
            src_ref=beams.at[flip(ma, d, n_ma), 0, 0, :, pl.ds(part * half + chunk * LANES, LANES)],
            dst_ref=ext[chunk].at[REACH + flip(ma, d, n_ma), :, pl.ds(part * LANES, LANES)],
            send_sem=a_send.at[chunk, d - 1, part],
            recv_sem=a_recv.at[chunk, d - 1, part],
            device_id=(flip(ma, d, n_ma), af),
            device_id_type=MESH,
        )

    def local(chunk, part):
        return pltpu.make_async_copy(
            beams.at[ma, 0, 0, :, pl.ds(part * half + chunk * LANES, LANES)],
            ext[chunk].at[REACH + ma, :, pl.ds(part * LANES, LANES)],
            own_sem.at[chunk, part],
        )

    def down(chunk):
        return pltpu.make_async_remote_copy(
            src_ref=ext[chunk].at[pl.ds(REACH, REACH)],
            dst_ref=ext[chunk].at[pl.ds(REACH + chans, REACH)],
            send_sem=h_send.at[chunk, 0],
            recv_sem=h_recv.at[chunk, 0],
            device_id=(ma, af - 1),
            device_id_type=MESH,
        )

    def up(chunk):
        return pltpu.make_async_remote_copy(
            src_ref=ext[chunk].at[pl.ds(chans, REACH)],
            dst_ref=ext[chunk].at[pl.ds(0, REACH)],
            send_sem=h_send.at[chunk, 1],
            recv_sem=h_recv.at[chunk, 1],
            device_id=(ma, af + 1),
            device_id_type=MESH,
        )

    parts = [(d, part) for d in range(1, n_ma) for part in range(2)]

    def launch(chunk):
        for d, part in parts:
            remote(chunk, d, part).start()
        for part in range(2):
            local(chunk, part).start()

    barrier = pltpu.get_barrier_semaphore()
    for d in range(1, n_ma):
        pl.semaphore_signal(barrier, inc=1, device_id=(flip(ma, d, n_ma), af), device_id_type=MESH)

    @pl.when(has_below)
    def _():
        pl.semaphore_signal(barrier, inc=1, device_id=(ma, af - 1), device_id_type=MESH)

    @pl.when(has_above)
    def _():
        pl.semaphore_signal(barrier, inc=1, device_id=(ma, af + 1), device_id_type=MESH)

    peers = n_ma - 1 + has_below.astype(jnp.int32) + has_above.astype(jnp.int32)
    pl.semaphore_wait(barrier, peers)

    for chunk in range(min(AHEAD, chunks)):
        launch(chunk)

    def forward(chunk):
        for d, part in parts:
            arriving(chunk, d, part).wait_recv()
        for part in range(2):
            local(chunk, part).wait()

        @pl.when(has_below)
        def _():
            down(chunk).start()

        @pl.when(has_above)
        def _():
            up(chunk).start()

    def halo_wait(chunk):
        @pl.when(has_above)
        def _():
            down(chunk).wait_recv()

        @pl.when(has_below)
        def _():
            up(chunk).wait_recv()

    def to_hbm(item):
        return pltpu.make_async_copy(
            stage.at[item % STAGES], out.at[0, item // slots, item % slots], out_sem.at[item % STAGES]
        )

    def compute(chunk):
        data = ext[chunk]
        first, last = chunk == 0, chunk == chunks - 1

        @pl.loop(0, chans * slots)
        def _(item):
            channel = item // slots
            slot = item % slots
            where = jnp.clip(partners[channel, slot] - af * chans + REACH, 0, chans + 2 * REACH - 1)
            right = data[where]
            own = data[REACH + channel]
            every = spectrum[channel, :, chunk * LANES : (chunk + 1) * LANES]
            weights = every[:1]
            for other in range(1, slots):
                weights = jnp.where(slot == other, every[other : other + 1], weights)
            real = own[:, :LANES].astype(jnp.float32) * weights
            imag = own[:, LANES:].astype(jnp.float32) * weights
            upper = jnp.concatenate([real, imag], axis=1).astype(jnp.bfloat16)
            lower = jnp.concatenate([imag, -real], axis=1).astype(jnp.bfloat16)
            if last:
                @pl.when(item >= STAGES)
                def _():
                    to_hbm(item - STAGES).wait()

            for index, left in enumerate((upper, lower)):
                product = lax.dot_general(
                    left, right, (((1,), (1,)), ((), ())), preferred_element_type=jnp.float32
                )
                if not first:
                    product = product + acc[item, index]
                if last:
                    stage[item % STAGES, index] = product.astype(jnp.bfloat16)
                else:
                    acc[item, index] = product
            if last:
                to_hbm(item).start()

    for chunk in range(chunks):
        forward(chunk)
        if chunk + AHEAD < chunks:
            launch(chunk + AHEAD)
        if chunk > 0:
            halo_wait(chunk - 1)
            compute(chunk - 1)
    halo_wait(chunks - 1)
    compute(chunks - 1)

    for item in range(chans * slots - STAGES, chans * slots):
        to_hbm(item).wait()
    for chunk in range(chunks):
        for d, part in parts:
            remote(chunk, d, part).wait_send()

        @pl.when(has_below)
        def _():
            down(chunk).wait_send()

        @pl.when(has_above)
        def _():
            up(chunk).wait_send()


def solution(mesh):
    n_ma, n_af = mesh.shape["ma"], mesh.shape["af"]

    def body(beams, spectrum, partners):
        rows, width = beams.shape[3], beams.shape[4]
        chans, slots = partners.shape
        chunks = width // 2 // LANES
        chunk_shape = (chans + 2 * REACH, rows, 2 * LANES)
        flops = 2 * chans * slots * 2 * rows * rows * width
        return pl.pallas_call(
            functools.partial(kernel, n_ma, n_af, chunks),
            out_shape=jax.ShapeDtypeStruct((1, chans, slots, 2, rows, rows), jnp.bfloat16),
            in_specs=[
                pl.BlockSpec(memory_space=pltpu.SMEM),
                pl.BlockSpec(memory_space=pl.ANY),
                pl.BlockSpec(memory_space=pltpu.VMEM),
            ],
            out_specs=pl.BlockSpec(memory_space=pl.ANY),
            scratch_shapes=[pltpu.VMEM(chunk_shape, jnp.bfloat16) for _ in range(chunks)]
            + [
                pltpu.VMEM((chans * slots, 2, rows, rows), jnp.float32),
                pltpu.VMEM((STAGES, 2, rows, rows), jnp.bfloat16),
                pltpu.SemaphoreType.DMA((chunks, n_ma - 1, 2)),
                pltpu.SemaphoreType.DMA((chunks, n_ma - 1, 2)),
                pltpu.SemaphoreType.DMA((chunks, 2)),
                pltpu.SemaphoreType.DMA((chunks, 2)),
                pltpu.SemaphoreType.DMA((chunks, 2)),
                pltpu.SemaphoreType.DMA((STAGES,)),
            ],
            compiler_params=pltpu.CompilerParams(
                collective_id=0, has_side_effects=True, vmem_limit_bytes=58 * 2**20
            ),
            cost_estimate=pl.CostEstimate(flops=flops, bytes_accessed=28 * 2**20, transcendentals=0),
        )(partners, beams, spectrum)

    in_specs = (P(None, "af", "ma", None, None), P("af", None, None), P("af", None))
    out_specs = P("ma", "af", None, None, None, None)
    return jax.shard_map(body, mesh=mesh, in_specs=in_specs, out_specs=out_specs, check_vma=False)
```

time: 342 us -> 127 us (0.37)
  Pallas kernels: 0 us -> 114 us
  blocking collectives: 100 us -> 0 us
  waiting for transfers between devices: 92 us -> 0 us
  matrix products: 66.4 us -> 0 us
  other arithmetic: 42.2 us -> 0 us
  loops' own time: 14.4 us -> 0 us
  starting transfers between devices: 7.96 us -> 0 us
  local copies, waits for them, and re-layouts: 17.6 us -> 11.9 us
    pallas_call x0 -> x1, Pallas kernels: none -> 114 us  [body(): pl.pallas_call(functools.partial(kernel, n_ma, n_af, chunks), out_shape=j...]
    all_to_all x1 -> x0, blocking collectives: 100 us -> none  [body(): moved = lax.all_to_all(beams, 'ma', split_axis=0, concat_axis=2, tiled=True)]
    ppermute x2 -> x0, waiting for transfers between devices: 92 us -> none  [from_behind(): return lax.ppermute(array, axis, pairs)]
    dot_general x12 -> x0, matrix products: 66.4 us -> none  [sandwich(): lax.dot_general(left, right, (((1,), (1,)), ((), ())), preferred_element_...]
    squeeze x1 -> x0, other arithmetic: 17.5 us -> none  [body(): beside_all = extended[0]]
    another operation x4 -> x0, other arithmetic: 16.5 us -> none
    another operation x1 -> x0, loops' own time: 14.4 us -> none  [body(): results = [lax.map(one_channel, jnp.arange(chans, dtype=jnp.int32))]]
    unnamed x0 -> x2, local copies, waits for them, and re-layouts: none -> 11.9 us
  transfers between devices with their start and end apart: 2 -> 0, of which waited for: 2 -> 0; matrix products, arithmetic and copies ran while one was open for 0% -> 0% of each run, Pallas kernels for 0% -> 0%
where the time goes in v1:
time: 127 us; the launch traced here: 126 us
  Pallas kernels  114 us (90%)
  local copies, waits for them, and re-layouts  11.9 us (9%)
    pallas_call x1, Pallas kernels, body(): pl.pallas_call(functools.partial(kernel, n_ma, n_af, chunks), out_shape=j...  114 us
    unnamed x2, local copies, waits for them, and re-layouts  11.9 us

profile of v1, /device:TPU:1, one launch (start us, length us, event | category | flops | bytes accessed | tf_op | source)
XLA Modules:
  0.0 126.3 jit_solution(17211197063077174313)
XLA Ops:
  0.0 1.5 %copy.4.spectrum = f32[4,3,1024]{2,1,0:T(4,128)} copy(f32[4,3,1024]{2,0,1:T(4,128)} %param.4) | data formatting | bytes 98304 | tf_op args[1]
  1.5 114.4 %shard_map.37 = bf16[1,4,3,2,512,512]{5,4,3,2,1,0:T(8,128)(2,1)} custom-call(s32[4,3]{1,0:T(4,128)} %partners.1, bf16[4,1,1,512,2048]{4,3,2,1,0:T(8,128)(2,1)} %beams.1, f32[4,3,1024]{2,1,0:T(4,128)} %copy.4.spectrum), custom_call_target="tpu_custom_call" | custom-call | flops 25769803776 | bytes 29360128 | tf_op jit(solution)/shard_map/pallas_call | solution.py:211
  115.8 10.5 %copy.6 = bf16[1,4,3,2,512,512]{5,4,3,2,1,0:T(8,128)(2,1)} copy(bf16[1,4,3,2,512,512]{5,4,3,2,1,0:T(8,128)(2,1)} %shard_map.37) | data formatting | bytes 25165824
